TPU v7x, 32 devices: a whole 2x2x4 slice. The times are simulated.
32 devices in a mesh: grid: 2 (over x), rank: 4 (over y, core), term: 4 (over z).
Axes of the slice: x: 2, y: 2, z: 4, core: 2. Of those that a mesh axis runs over, the one named last changes fastest.
Arguments:
- rhs: float32 [128, 4, 256], P('rank', 'grid')
- coef: float32 [12, 4, 256], P('term', 'grid'), may hold values from 0.03 to 0.3
- env: float32 [12, 128, 128], P('term', 'rank'), as said below
Outputs:
- solution: float32 [128, 4, 256], P('rank', 'grid')
- residual: float32 [128, 4, 256], P('rank', 'grid')
Inputs may be any that keep to these rules, and one draw needn't show every extreme that they name: env[k] is a symmetric matrix for every k.
All inputs are finite; a program needn't handle non-finite values.
Results may differ from a plain program's by a relative error of at most 0.0003.
Values sent between devices are 32-bit elements; how exact they have to be, the bound alone decides.
A program may use at most 64 MiB of HBM per device.

v0:
```python
import jax
import jax.numpy as jnp
from jax import lax
from jax.sharding import PartitionSpec as P

ITERS = 4


def padded_2(block, sides, width):
    for axis, dim in sides:
        count = lax.axis_size(axis)
        forward = [(i, i + 1) for i in range(count - 1)]
        backward = [(target, source) for source, target in forward]
        low = lax.ppermute(
            lax.slice_in_dim(block, block.shape[dim] - width, None, axis=dim), axis, forward
        )
        high = lax.ppermute(lax.slice_in_dim(block, 0, width, axis=dim), axis, backward)
        block = jnp.concatenate([low, block, high], axis=dim)
    return block


def face_weights(padded):
    wide = jnp.pad(padded, ((0, 0), (0, 0), (1, 1)))
    centre = wide[:, 1:-1, 1:-1]
    face_up = 0.5 * (centre + wide[:, 2:, 1:-1])
    face_down = 0.5 * (centre + wide[:, :-2, 1:-1])
    face_right = 0.5 * (centre + wide[:, 1:-1, 2:])
    face_left = 0.5 * (centre + wide[:, 1:-1, :-2])
    return (face_up + face_down + face_right + face_left, face_up, face_down, face_right, face_left)


def apply_faces(field, faces):
    middle = field[..., 1:-1, :]
    sideways = jnp.pad(middle, [(0, 0)] * (middle.ndim - 1) + [(1, 1)])
    total, face_up, face_down, face_right, face_left = faces
    return (
        total * middle
        - face_up * field[..., 2:, :]
        - face_down * field[..., :-2, :]
        - face_right * sideways[..., 2:]
        - face_left * sideways[..., :-2]
    )


def shards(rhs, coef, env):
    coef_padded = padded_2(coef, (("grid", 1),), 1)
    faces = tuple((weights[:, None] for weights in face_weights(coef_padded)))

    def square_sum(vector):
        return lax.psum(jnp.sum(vector * vector), ("grid", "rank"))

    solution = jnp.zeros(rhs.shape, jnp.float32)
    residual = rhs
    direction = rhs
    norm_now = square_sum(residual)
    for step in range(ITERS):
        padded = padded_2(direction, (("grid", 1),), 1)
        stenciled = apply_faces(padded[None], faces)
        image = lax.psum_scatter(
            jnp.einsum("krs,krxy->sxy", env, stenciled, precision=lax.Precision.HIGHEST),
            "rank",
            scatter_dimension=0,
            tiled=True,
        )
        image = lax.psum(image, "term")
        alpha = norm_now / lax.psum(jnp.sum(direction * image), ("grid", "rank"))
        solution = solution + alpha * direction
        residual = residual - alpha * image
        norm_next = square_sum(residual)
        direction = residual + norm_next / norm_now * direction
        norm_now = norm_next
    return (solution, residual)


def solution(mesh):
    placed = (P("rank", "grid", None), P("term", "grid", None), P("term", "rank", None))
    return jax.shard_map(
        shards,
        mesh=mesh,
        in_specs=placed,
        out_specs=(P("rank", "grid", None), P("rank", "grid", None)),
        check_vma=False,
    )
```

profile of v0, /device:TPU:0, one launch (start us, length us, event | category | flops | bytes accessed | tf_op | source)
XLA Modules:
  0.0 443.1 jit_solution(13769848011755938709)
XLA Ops:
  8.0 4.8 %collective-permute-start.1 = (f32[3,1,256]{2,1,0:T(1,128)S(1)}, f32[3,1,256]{2,1,0:T(1,128)S(1)}, u32[]{:S(2)}, u32[]{:S(2)}) collective-permute-start(f32[3,1,256]{2,1,0:T(1,128)S(1)} %get-tuple-element.49), channel_id=1, source_target_pairs={{0,16},{1,17},{2,18},{3,19},{4,20},{5,21},{6,22},{7,23},{8,24},{9,... | collective-permute-start | bytes 9224 | tf_op jit(solution)/shard_map/ppermute | solution.py:14
  15.1 4.5 %collective-permute-start.2 = (f32[32,1,256]{2,1,0:T(1,128)S(1)}, f32[32,1,256]{2,1,0:T(1,128)S(1)}, u32[]{:S(2)}, u32[]{:S(2)}) collective-permute-start(f32[32,1,256]{2,1,0:T(1,128)S(1)} %get-tuple-element.47), channel_id=1, source_target_pairs={{0,16},{1,17},{2,18},{3,19},{4,20},{5,21},{6,22},{7,23},{8,24},{9,... | collective-permute-start | bytes 98312 | tf_op jit(solution)/shard_map/ppermute | solution.py:14
  21.3 4.2 collective-permute-done.3
  29.4 30.5 %all-reduce.27.cloned.1.call-done = f32[128,2,256]{2,1,0:T(2,128)} async-done(((f32[128,2,256]{2,1,0:T(2,128)}), f32[128,2,256]{2,1,0:T(2,128)}) %all-reduce.27.cloned.1.call-update) | async-done | bytes 262160
  61.4 35.5 %all-reduce.19.cloned.1.call-done = f32[32,2,256]{2,1,0:T(2,128)} async-done(((f32[32,2,256]{2,1,0:T(2,128)}), f32[32,2,256]{2,1,0:T(2,128)}) %all-reduce.19.cloned.1.call-update) | async-done | bytes 65552 | tf_op jit(solution)/shard_map/psum | solution.py:65
  98.5 12.5 %all-reduce.9 = (f32[]{:T(128)}, f32[]{:T(128)}) all-reduce(f32[]{:T(128)} %get-tuple-element.5, f32[]{:T(128)} %get-tuple-element.4), channel_id=1, replica_groups=mesh['grid'=2,'rank'=4,'term'=4] {'grid','rank'}, use_global_device_ids=true, to_apply=%region_1.2 | all-reduce | flops 2 | bytes 16 | tf_op jit(solution)/shard_map/psum | solution.py:50
  113.0 12.5 %psum.87 = f32[]{:T(128)} all-reduce(f32[]{:T(128)} %multiply_reduce_fusion.5), channel_id=1, replica_groups=mesh['grid'=2,'rank'=4,'term'=4] {'grid','rank'}, use_global_device_ids=true, to_apply=%region_7.8 | all-reduce | flops 1 | bytes 8 | tf_op jit(solution)/shard_map/psum | solution.py:50
  126.9 3.4 collective-permute-start.4
  131.9 4.2 collective-permute-done.5
  137.8 30.0 %all-reduce.29.cloned.1.call-done = f32[128,2,256]{2,1,0:T(2,128)} async-done(((f32[128,2,256]{2,1,0:T(2,128)}), f32[128,2,256]{2,1,0:T(2,128)}) %all-reduce.29.cloned.1.call-update) | async-done | bytes 262160
  169.3 35.3 %all-reduce.21.cloned.1.call-done = f32[32,2,256]{2,1,0:T(2,128)} async-done(((f32[32,2,256]{2,1,0:T(2,128)}), f32[32,2,256]{2,1,0:T(2,128)}) %all-reduce.21.cloned.1.call-update) | async-done | bytes 65552 | tf_op jit(solution)/shard_map/psum | solution.py:65
  206.2 12.5 %psum.89 = f32[]{:T(128)} all-reduce(f32[]{:T(128)} %multiply_reduce_fusion.4), channel_id=1, replica_groups=mesh['grid'=2,'rank'=4,'term'=4] {'grid','rank'}, use_global_device_ids=true, to_apply=%region_11.12 | all-reduce | flops 1 | bytes 8 | tf_op jit(solution)/shard_map/psum | solution.py:66
  220.7 12.4 %psum.90 = f32[]{:T(128)} all-reduce(f32[]{:T(128)} %get-tuple-element.10), channel_id=1, replica_groups=mesh['grid'=2,'rank'=4,'term'=4] {'grid','rank'}, use_global_device_ids=true, to_apply=%region_13.14 | all-reduce | flops 1 | bytes 8 | tf_op jit(solution)/shard_map/psum | solution.py:50
  234.6 3.4 collective-permute-start.6
  239.6 4.2 collective-permute-done.7
  245.5 30.0 %all-reduce.31.cloned.1.call-done = f32[128,2,256]{2,1,0:T(2,128)} async-done(((f32[128,2,256]{2,1,0:T(2,128)}), f32[128,2,256]{2,1,0:T(2,128)}) %all-reduce.31.cloned.1.call-update) | async-done | bytes 262160
  277.0 35.3 %all-reduce.23.cloned.1.call-done = f32[32,2,256]{2,1,0:T(2,128)} async-done(((f32[32,2,256]{2,1,0:T(2,128)}), f32[32,2,256]{2,1,0:T(2,128)}) %all-reduce.23.cloned.1.call-update) | async-done | bytes 65552 | tf_op jit(solution)/shard_map/psum | solution.py:65
  313.9 12.5 %psum.92 = f32[]{:T(128)} all-reduce(f32[]{:T(128)} %multiply_reduce_fusion.2), channel_id=1, replica_groups=mesh['grid'=2,'rank'=4,'term'=4] {'grid','rank'}, use_global_device_ids=true, to_apply=%region_17.18 | all-reduce | flops 1 | bytes 8 | tf_op jit(solution)/shard_map/psum | solution.py:66
  328.4 12.5 %psum.93 = f32[]{:T(128)} all-reduce(f32[]{:T(128)} %get-tuple-element.8), channel_id=1, replica_groups=mesh['grid'=2,'rank'=4,'term'=4] {'grid','rank'}, use_global_device_ids=true, to_apply=%region_19.20 | all-reduce | flops 1 | bytes 8 | tf_op jit(solution)/shard_map/psum | solution.py:50
  342.3 3.4 collective-permute-start.8
  347.3 4.2 collective-permute-done.9
  353.2 30.0 %all-reduce.33.cloned.1.call-done = f32[128,2,256]{2,1,0:T(2,128)} async-done(((f32[128,2,256]{2,1,0:T(2,128)}), f32[128,2,256]{2,1,0:T(2,128)}) %all-reduce.33.cloned.1.call-update) | async-done | bytes 262160
  384.6 35.5 %all-reduce.25.cloned.1.call-done = f32[32,2,256]{2,1,0:T(2,128)} async-done(((f32[32,2,256]{2,1,0:T(2,128)}), f32[32,2,256]{2,1,0:T(2,128)}) %all-reduce.25.cloned.1.call-update) | async-done | bytes 65552 | tf_op jit(solution)/shard_map/psum | solution.py:65
  421.7 12.5 %psum.95 = f32[]{:T(128)} all-reduce(f32[]{:T(128)} %multiply_reduce_fusion), channel_id=1, replica_groups=mesh['grid'=2,'rank'=4,'term'=4] {'grid','rank'}, use_global_device_ids=true, to_apply=%region_23.24 | all-reduce | flops 1 | bytes 8 | tf_op jit(solution)/shard_map/psum | solution.py:66
  (105 shorter events, 32.7 us)
Async XLA Ops:
  7.2 18.8 %copy-start = (f32[3,32,128]{2,1,0:T(8,128)S(1)}, f32[3,32,128]{2,1,0:T(8,128)}, u32[]{:S(2)}) copy-start(f32[3,32,128]{2,1,0:T(8,128)} %param.5) | copy-start | bytes 147460
  7.2 52.7 %all-reduce.27.cloned.1.call-start = ((), (), s32[]{:S(2)}) async-start(), calls=%async_computation.4 | async-start | bytes 524288
  8.0 13.0 %collective-permute-start.1 = (f32[3,1,256]{2,1,0:T(1,128)S(1)}, f32[3,1,256]{2,1,0:T(1,128)S(1)}, u32[]{:S(2)}, u32[]{:S(2)}) collective-permute-start(f32[3,1,256]{2,1,0:T(1,128)S(1)} %get-tuple-element.49), channel_id=1, source_target_pairs={{0,16},{1,17},{2,18},{3,19},{4,20},{5,21},{6,22},{7,23},{8,24},{9,... | collective-permute-start | bytes 9224 | tf_op jit(solution)/shard_map/ppermute | solution.py:14
  12.8 8.2 %collective-permute-start = (f32[3,1,256]{2,1,0:T(1,128)S(1)}, f32[3,1,256]{2,1,0:T(1,128)S(1)}, u32[]{:S(2)}, u32[]{:S(2)}) collective-permute-start(f32[3,1,256]{2,1,0:T(1,128)S(1)} %get-tuple-element.50), channel_id=1, source_target_pairs={{16,0},{17,1},{18,2},{19,3},{20,4},{21,5},{22,6},{23,7},{24,8},{25... | collective-permute-start | bytes 9224 | tf_op jit(solution)/shard_map/ppermute | solution.py:17
  14.1 6.9 %copy-start.6 = (f32[3,2,256]{2,1,0:T(2,128)S(1)}, f32[3,2,256]{2,1,0:T(2,128)}, u32[]{:S(2)}) copy-start(f32[3,2,256]{2,1,0:T(2,128)} %param.4) | copy-start | bytes 18436
  15.1 6.1 %collective-permute-start.2 = (f32[32,1,256]{2,1,0:T(1,128)S(1)}, f32[32,1,256]{2,1,0:T(1,128)S(1)}, u32[]{:S(2)}, u32[]{:S(2)}) collective-permute-start(f32[32,1,256]{2,1,0:T(1,128)S(1)} %get-tuple-element.47), channel_id=1, source_target_pairs={{0,16},{1,17},{2,18},{3,19},{4,20},{5,21},{6,22},{7,23},{8,24},{9,... | collective-permute-start | bytes 98312 | tf_op jit(solution)/shard_map/ppermute | solution.py:14
  19.7 5.8 %collective-permute-start.3 = (f32[32,1,256]{2,1,0:T(1,128)S(1)}, f32[32,1,256]{2,1,0:T(1,128)S(1)}, u32[]{:S(2)}, u32[]{:S(2)}) collective-permute-start(f32[32,1,256]{2,1,0:T(1,128)S(1)} %get-tuple-element.48), channel_id=1, source_target_pairs={{16,0},{17,1},{18,2},{19,3},{20,4},{21,5},{22,6},{23,7},{24,8},{25... | collective-permute-start | bytes 98312 | tf_op jit(solution)/shard_map/ppermute | solution.py:17
  27.4 69.5 %all-reduce.19.cloned.1.call-start = ((), (), s32[]{:S(2)}) async-start(), calls=%async_computation | async-start | bytes 131072 | tf_op jit(solution)/shard_map/psum | solution.py:65
  61.4 106.4 %all-reduce.29.cloned.1.call-start = ((), (), s32[]{:S(2)}) async-start(), calls=%async_computation.5 | async-start | bytes 524288
  96.9 15.4 %copy-start.2 = (f32[32,2,256]{2,1,0:T(2,128)S(1)}, f32[32,2,256]{2,1,0:T(2,128)}, u32[]{:S(2)}) copy-start(f32[32,2,256]{2,1,0:T(2,128)} %all-reduce.19.cloned.1.call-done) | copy-start | bytes 196612
  126.9 4.9 %collective-permute-start.4 = (f32[32,1,256]{2,1,0:T(1,128)S(1)}, f32[32,1,256]{2,1,0:T(1,128)S(1)}, u32[]{:S(2)}, u32[]{:S(2)}) collective-permute-start(f32[32,1,256]{2,1,0:T(1,128)S(1)} %get-tuple-element.43), channel_id=1, source_target_pairs={{0,16},{1,17},{2,18},{3,19},{4,20},{5,21},{6,22},{7,23},{8,24},{9,... | collective-permute-start | bytes 98312 | tf_op jit(solution)/shard_map/ppermute | solution.py:14
  130.3 5.8 %collective-permute-start.5 = (f32[32,1,256]{2,1,0:T(1,128)S(1)}, f32[32,1,256]{2,1,0:T(1,128)S(1)}, u32[]{:S(2)}, u32[]{:S(2)}) collective-permute-start(f32[32,1,256]{2,1,0:T(1,128)S(1)} %get-tuple-element.44), channel_id=1, source_target_pairs={{16,0},{17,1},{18,2},{19,3},{20,4},{21,5},{22,6},{23,7},{24,8},{25... | collective-permute-start | bytes 98312 | tf_op jit(solution)/shard_map/ppermute | solution.py:17
  137.7 66.9 %all-reduce.21.cloned.1.call-start = ((), (), s32[]{:S(2)}) async-start(), calls=%async_computation.1 | async-start | bytes 131072 | tf_op jit(solution)/shard_map/psum | solution.py:65
  169.2 106.2 %all-reduce.31.cloned.1.call-start = ((), (), s32[]{:S(2)}) async-start(), calls=%async_computation.6 | async-start | bytes 524288
  204.6 15.4 %copy-start.4 = (f32[32,2,256]{2,1,0:T(2,128)S(1)}, f32[32,2,256]{2,1,0:T(2,128)}, u32[]{:S(2)}) copy-start(f32[32,2,256]{2,1,0:T(2,128)} %all-reduce.21.cloned.1.call-done) | copy-start | bytes 196612
  234.6 4.9 %collective-permute-start.6 = (f32[32,1,256]{2,1,0:T(1,128)S(1)}, f32[32,1,256]{2,1,0:T(1,128)S(1)}, u32[]{:S(2)}, u32[]{:S(2)}) collective-permute-start(f32[32,1,256]{2,1,0:T(1,128)S(1)} %get-tuple-element.39), channel_id=1, source_target_pairs={{0,16},{1,17},{2,18},{3,19},{4,20},{5,21},{6,22},{7,23},{8,24},{9,... | collective-permute-start | bytes 98312 | tf_op jit(solution)/shard_map/ppermute | solution.py:14
  238.0 5.8 %collective-permute-start.7 = (f32[32,1,256]{2,1,0:T(1,128)S(1)}, f32[32,1,256]{2,1,0:T(1,128)S(1)}, u32[]{:S(2)}, u32[]{:S(2)}) collective-permute-start(f32[32,1,256]{2,1,0:T(1,128)S(1)} %get-tuple-element.40), channel_id=1, source_target_pairs={{16,0},{17,1},{18,2},{19,3},{20,4},{21,5},{22,6},{23,7},{24,8},{25... | collective-permute-start | bytes 98312 | tf_op jit(solution)/shard_map/ppermute | solution.py:17
  245.4 66.9 %all-reduce.23.cloned.1.call-start = ((), (), s32[]{:S(2)}) async-start(), calls=%async_computation.2 | async-start | bytes 131072 | tf_op jit(solution)/shard_map/psum | solution.py:65
  276.9 106.2 %all-reduce.33.cloned.1.call-start = ((), (), s32[]{:S(2)}) async-start(), calls=%async_computation.7 | async-start | bytes 524288
  312.3 15.4 %copy-start.3 = (f32[32,2,256]{2,1,0:T(2,128)S(1)}, f32[32,2,256]{2,1,0:T(2,128)}, u32[]{:S(2)}) copy-start(f32[32,2,256]{2,1,0:T(2,128)} %all-reduce.23.cloned.1.call-done) | copy-start | bytes 196612
  342.3 4.9 %collective-permute-start.8 = (f32[32,1,256]{2,1,0:T(1,128)S(1)}, f32[32,1,256]{2,1,0:T(1,128)S(1)}, u32[]{:S(2)}, u32[]{:S(2)}) collective-permute-start(f32[32,1,256]{2,1,0:T(1,128)S(1)} %get-tuple-element.35), channel_id=1, source_target_pairs={{0,16},{1,17},{2,18},{3,19},{4,20},{5,21},{6,22},{7,23},{8,24},{9,... | collective-permute-start | bytes 98312 | tf_op jit(solution)/shard_map/ppermute | solution.py:14
  345.7 5.8 %collective-permute-start.9 = (f32[32,1,256]{2,1,0:T(1,128)S(1)}, f32[32,1,256]{2,1,0:T(1,128)S(1)}, u32[]{:S(2)}, u32[]{:S(2)}) collective-permute-start(f32[32,1,256]{2,1,0:T(1,128)S(1)} %get-tuple-element.36), channel_id=1, source_target_pairs={{16,0},{17,1},{18,2},{19,3},{20,4},{21,5},{22,6},{23,7},{24,8},{25... | collective-permute-start | bytes 98312 | tf_op jit(solution)/shard_map/ppermute | solution.py:17
  353.1 67.0 %all-reduce.25.cloned.1.call-start = ((), (), s32[]{:S(2)}) async-start(), calls=%async_computation.3 | async-start | bytes 131072 | tf_op jit(solution)/shard_map/psum | solution.py:65
  420.1 15.4 %copy-start.5 = (f32[32,2,256]{2,1,0:T(2,128)S(1)}, f32[32,2,256]{2,1,0:T(2,128)}, u32[]{:S(2)}) copy-start(f32[32,2,256]{2,1,0:T(2,128)} %all-reduce.25.cloned.1.call-done) | copy-start | bytes 196612
  (2 other events, 5.0 us)
Sparse Core Ops, SparseCore 0:
  27.6 32.2 all-reduce.26
  62.9 33.9 all-reduce.18
  137.9 29.8 all-reduce.28
  170.6 33.9 all-reduce.20
  245.5 29.8 all-reduce.30
  278.3 33.9 all-reduce.22
  353.2 29.8 all-reduce.32
  386.1 33.9 all-reduce.24
where the time goes:
time: 444 us; the launch traced here: 443 us
  waiting for transfers between devices  280 us (63%)
  blocking collectives  87.3 us (20%)
  starting transfers between devices  26.2 us (6%)
  between operations  24.8 us (6%)
  local copies, waits for them, and re-layouts  13.1 us (3%)
  other arithmetic  9.37 us (2%)
    psum x4, waiting for transfers between devices, shards(): image = lax.psum(image, 'term')  142 us
    unnamed x12, waiting for transfers between devices  121 us
    psum x4, blocking collectives, square_sum(): return lax.psum(jnp.sum(vector * vector), ('grid', 'rank'))  49.9 us
    psum x3, blocking collectives, shards(): alpha = norm_now / lax.psum(jnp.sum(direction * image), ('grid', 'rank'))  37.4 us
    ppermute x5, starting transfers between devices, padded_2(): lax.ppermute(lax.slice_in_dim(block, block.shape[dim] - width, None, axis...  19.4 us
    ppermute x5, waiting for transfers between devices, padded_2(): lax.ppermute(lax.slice_in_dim(block, 0, width, axis=dim), axis, backward)  16.9 us
  transfers between devices with their start and end apart: 18, of which 15 were waited for; matrix products, arithmetic and copies ran while one was open for 0% of the time, Pallas kernels for 0%

commit v1 on v0

--- a/solution.py
+++ b/solution.py
@@ -62,7 +62,15 @@
             scatter_dimension=0,
             tiled=True,
         )
-        image = lax.psum(image, "term")
+        n = jax.lax.psum(1, "term")
+        b_next, piece_out = (image, 0)
+        while 1 << piece_out < n:
+            value_now = jax.lax.ppermute(
+                b_next, "term", tuple(((c, c ^ 1 << piece_out) for c in range(n)))
+            )
+            b_next = b_next + value_now
+            piece_out = piece_out + 1
+        image = b_next
         alpha = norm_now / lax.psum(jnp.sum(direction * image), ("grid", "rank"))
         solution = solution + alpha * direction
         residual = residual - alpha * image

time: 444 us -> 342 us (0.77)
  waiting for transfers between devices: 280 us -> 166 us
  starting transfers between devices: 26.2 us -> 42 us
    psum x4 -> x0, waiting for transfers between devices: 142 us -> none  [shards(): image = lax.psum(image, 'term')]
    ppermute x0 -> x8, waiting for transfers between devices: none -> 22.1 us  [shards(): jax.lax.ppermute(b_next, 'term', tuple(((c, c ^ 1 << piece_out) for c in...]
    ppermute x0 -> x8, starting transfers between devices: none -> 15.8 us  [shards(): jax.lax.ppermute(b_next, 'term', tuple(((c, c ^ 1 << piece_out) for c in...]
    unnamed x12 -> x8, waiting for transfers between devices: 121 us -> 126 us
  transfers between devices with their start and end apart: 18 -> 22, of which waited for: 15 -> 19; matrix products, arithmetic and copies ran while one was open for 0% -> 1% of each run, Pallas kernels for 0% -> 0%
where the time goes in v1:
time: 342 us; the launch traced here: 341 us
  waiting for transfers between devices  166 us (49%)
  blocking collectives  86.9 us (25%)
  starting transfers between devices  42 us (12%)
  between operations  24.2 us (7%)
  local copies, waits for them, and re-layouts  10.6 us (3%)
  other arithmetic  9.24 us (3%)
    unnamed x8, waiting for transfers between devices  126 us
    psum x4, blocking collectives, square_sum(): return lax.psum(jnp.sum(vector * vector), ('grid', 'rank'))  49.6 us
    psum x3, blocking collectives, shards(): alpha = norm_now / lax.psum(jnp.sum(direction * image), ('grid', 'rank'))  37.2 us
    ppermute x8, waiting for transfers between devices, shards(): jax.lax.ppermute(b_next, 'term', tuple(((c, c ^ 1 << piece_out) for c in...  22.1 us
    ppermute x5, starting transfers between devices, padded_2(): lax.ppermute(lax.slice_in_dim(block, block.shape[dim] - width, None, axis...  19.5 us
    ppermute x5, waiting for transfers between devices, padded_2(): lax.ppermute(lax.slice_in_dim(block, 0, width, axis=dim), axis, backward)  16.9 us
    ppermute x8, starting transfers between devices, shards(): jax.lax.ppermute(b_next, 'term', tuple(((c, c ^ 1 << piece_out) for c in...  15.8 us
  transfers between devices with their start and end apart: 22, of which 19 were waited for; matrix products, arithmetic and copies ran while one was open for 1% of the time, Pallas kernels for 0%

profile of v1, /device:TPU:0, one launch (start us, length us, event | category | flops | bytes accessed | tf_op | source)
XLA Modules:
  0.0 341.4 jit_solution(9862075367703886013)
XLA Ops:
  8.0 4.8 %collective-permute-start.1 = (f32[3,1,256]{2,1,0:T(1,128)S(1)}, f32[3,1,256]{2,1,0:T(1,128)S(1)}, u32[]{:S(2)}, u32[]{:S(2)}) collective-permute-start(f32[3,1,256]{2,1,0:T(1,128)S(1)} %get-tuple-element.56), channel_id=1, source_target_pairs={{0,16},{1,17},{2,18},{3,19},{4,20},{5,21},{6,22},{7,23},{8,24},{9,... | collective-permute-start | bytes 9224 | tf_op jit(solution)/shard_map/ppermute | solution.py:14
  15.1 4.5 %collective-permute-start.2 = (f32[32,1,256]{2,1,0:T(1,128)S(1)}, f32[32,1,256]{2,1,0:T(1,128)S(1)}, u32[]{:S(2)}, u32[]{:S(2)}) collective-permute-start(f32[32,1,256]{2,1,0:T(1,128)S(1)} %get-tuple-element.54), channel_id=1, source_target_pairs={{0,16},{1,17},{2,18},{3,19},{4,20},{5,21},{6,22},{7,23},{8,24},{9,... | collective-permute-start | bytes 98312 | tf_op jit(solution)/shard_map/ppermute | solution.py:14
  21.3 4.2 %collective-permute-done.3 = f32[32,1,256]{2,1,0:T(1,128)S(1)} collective-permute-done((f32[32,1,256]{2,1,0:T(1,128)S(1)}, f32[32,1,256]{2,1,0:T(1,128)S(1)}, u32[]{:S(2)}, u32[]{:S(2)}) %collective-permute-start.3) | collective-permute-done | bytes 32800 | tf_op jit(solution)/shard_map/ppermute | solution.py:17
  29.4 30.5 %all-reduce.15.cloned.1.call-done = f32[128,2,256]{2,1,0:T(2,128)} async-done(((f32[128,2,256]{2,1,0:T(2,128)}), f32[128,2,256]{2,1,0:T(2,128)}) %all-reduce.15.cloned.1.call-update) | async-done | bytes 262160
  62.2 2.8 collective-permute-done.4
  71.8 12.4 %all-reduce.9 = (f32[]{:T(128)}, f32[]{:T(128)}) all-reduce(f32[]{:T(128)} %get-tuple-element.5, f32[]{:T(128)} %get-tuple-element.4), channel_id=1, replica_groups=mesh['grid'=2,'rank'=4,'term'=4] {'grid','rank'}, use_global_device_ids=true, to_apply=%region_1.2 | all-reduce | flops 2 | bytes 16 | tf_op jit(solution)/shard_map/psum | solution.py:50
  86.2 12.4 %psum.58 = f32[]{:T(128)} all-reduce(f32[]{:T(128)} %multiply_reduce_fusion.5), channel_id=1, replica_groups=mesh['grid'=2,'rank'=4,'term'=4] {'grid','rank'}, use_global_device_ids=true, to_apply=%region_6.7 | all-reduce | flops 1 | bytes 8 | tf_op jit(solution)/shard_map/psum | solution.py:50
  100.1 3.4 collective-permute-start.6
  105.0 4.2 %collective-permute-done.7 = f32[32,1,256]{2,1,0:T(1,128)S(1)} collective-permute-done((f32[32,1,256]{2,1,0:T(1,128)S(1)}, f32[32,1,256]{2,1,0:T(1,128)S(1)}, u32[]{:S(2)}, u32[]{:S(2)}) %collective-permute-start.7) | collective-permute-done | bytes 32800 | tf_op jit(solution)/shard_map/ppermute | solution.py:17
  110.9 31.9 %all-reduce.17.cloned.1.call-done = f32[128,2,256]{2,1,0:T(2,128)} async-done(((f32[128,2,256]{2,1,0:T(2,128)}), f32[128,2,256]{2,1,0:T(2,128)}) %all-reduce.17.cloned.1.call-update) | async-done | bytes 262160
  145.1 2.8 collective-permute-done.8
  154.7 12.4 %psum.59 = f32[]{:T(128)} all-reduce(f32[]{:T(128)} %get-tuple-element.16), channel_id=1, replica_groups=mesh['grid'=2,'rank'=4,'term'=4] {'grid','rank'}, use_global_device_ids=true, to_apply=%region_9.10 | all-reduce | flops 1 | bytes 8 | tf_op jit(solution)/shard_map/psum | solution.py:74
  169.1 12.4 %psum.60 = f32[]{:T(128)} all-reduce(f32[]{:T(128)} %get-tuple-element.14), channel_id=1, replica_groups=mesh['grid'=2,'rank'=4,'term'=4] {'grid','rank'}, use_global_device_ids=true, to_apply=%region_11.12 | all-reduce | flops 1 | bytes 8 | tf_op jit(solution)/shard_map/psum | solution.py:50
  182.9 3.4 collective-permute-start.10
  187.9 4.2 %collective-permute-done.11 = f32[32,1,256]{2,1,0:T(1,128)S(1)} collective-permute-done((f32[32,1,256]{2,1,0:T(1,128)S(1)}, f32[32,1,256]{2,1,0:T(1,128)S(1)}, u32[]{:S(2)}, u32[]{:S(2)}) %collective-permute-start.11) | collective-permute-done | bytes 32800 | tf_op jit(solution)/shard_map/ppermute | solution.py:17
  193.8 31.8 %all-reduce.19.cloned.1.call-done = f32[128,2,256]{2,1,0:T(2,128)} async-done(((f32[128,2,256]{2,1,0:T(2,128)}), f32[128,2,256]{2,1,0:T(2,128)}) %all-reduce.19.cloned.1.call-update) | async-done | bytes 262160
  228.0 2.8 collective-permute-done.12
  237.6 12.4 %psum.61 = f32[]{:T(128)} all-reduce(f32[]{:T(128)} %get-tuple-element.12), channel_id=1, replica_groups=mesh['grid'=2,'rank'=4,'term'=4] {'grid','rank'}, use_global_device_ids=true, to_apply=%region_14.15 | all-reduce | flops 1 | bytes 8 | tf_op jit(solution)/shard_map/psum | solution.py:74
  252.0 12.4 %psum.62 = f32[]{:T(128)} all-reduce(f32[]{:T(128)} %get-tuple-element.10), channel_id=1, replica_groups=mesh['grid'=2,'rank'=4,'term'=4] {'grid','rank'}, use_global_device_ids=true, to_apply=%region_16.17 | all-reduce | flops 1 | bytes 8 | tf_op jit(solution)/shard_map/psum | solution.py:50
  265.8 3.4 collective-permute-start.14
  270.8 4.2 %collective-permute-done.15 = f32[32,1,256]{2,1,0:T(1,128)S(1)} collective-permute-done((f32[32,1,256]{2,1,0:T(1,128)S(1)}, f32[32,1,256]{2,1,0:T(1,128)S(1)}, u32[]{:S(2)}, u32[]{:S(2)}) %collective-permute-start.15) | collective-permute-done | bytes 32800 | tf_op jit(solution)/shard_map/ppermute | solution.py:17
  276.7 31.9 %all-reduce.21.cloned.1.call-done = f32[128,2,256]{2,1,0:T(2,128)} async-done(((f32[128,2,256]{2,1,0:T(2,128)}), f32[128,2,256]{2,1,0:T(2,128)}) %all-reduce.21.cloned.1.call-update) | async-done | bytes 262160
  310.9 2.8 collective-permute-done.16
  320.4 12.4 %psum.63 = f32[]{:T(128)} all-reduce(f32[]{:T(128)} %get-tuple-element.8), channel_id=1, replica_groups=mesh['grid'=2,'rank'=4,'term'=4] {'grid','rank'}, use_global_device_ids=true, to_apply=%region_19.20 | all-reduce | flops 1 | bytes 8 | tf_op jit(solution)/shard_map/psum | solution.py:74
  (105 shorter events, 56.7 us)
Async XLA Ops:
  7.2 18.8 %copy-start = (f32[3,32,128]{2,1,0:T(8,128)S(1)}, f32[3,32,128]{2,1,0:T(8,128)}, u32[]{:S(2)}) copy-start(f32[3,32,128]{2,1,0:T(8,128)} %param.5) | copy-start | bytes 147460
  7.2 52.7 %all-reduce.15.cloned.1.call-start = ((), (), s32[]{:S(2)}) async-start(), calls=%async_computation | async-start | bytes 524288
  8.0 13.0 %collective-permute-start.1 = (f32[3,1,256]{2,1,0:T(1,128)S(1)}, f32[3,1,256]{2,1,0:T(1,128)S(1)}, u32[]{:S(2)}, u32[]{:S(2)}) collective-permute-start(f32[3,1,256]{2,1,0:T(1,128)S(1)} %get-tuple-element.56), channel_id=1, source_target_pairs={{0,16},{1,17},{2,18},{3,19},{4,20},{5,21},{6,22},{7,23},{8,24},{9,... | collective-permute-start | bytes 9224 | tf_op jit(solution)/shard_map/ppermute | solution.py:14
  12.8 8.2 %collective-permute-start = (f32[3,1,256]{2,1,0:T(1,128)S(1)}, f32[3,1,256]{2,1,0:T(1,128)S(1)}, u32[]{:S(2)}, u32[]{:S(2)}) collective-permute-start(f32[3,1,256]{2,1,0:T(1,128)S(1)} %get-tuple-element.57), channel_id=1, source_target_pairs={{16,0},{17,1},{18,2},{19,3},{20,4},{21,5},{22,6},{23,7},{24,8},{25... | collective-permute-start | bytes 9224 | tf_op jit(solution)/shard_map/ppermute | solution.py:17
  14.1 6.9 %copy-start.2 = (f32[3,2,256]{2,1,0:T(2,128)S(1)}, f32[3,2,256]{2,1,0:T(2,128)}, u32[]{:S(2)}) copy-start(f32[3,2,256]{2,1,0:T(2,128)} %param.4) | copy-start | bytes 18436
  15.1 6.1 %collective-permute-start.2 = (f32[32,1,256]{2,1,0:T(1,128)S(1)}, f32[32,1,256]{2,1,0:T(1,128)S(1)}, u32[]{:S(2)}, u32[]{:S(2)}) collective-permute-start(f32[32,1,256]{2,1,0:T(1,128)S(1)} %get-tuple-element.54), channel_id=1, source_target_pairs={{0,16},{1,17},{2,18},{3,19},{4,20},{5,21},{6,22},{7,23},{8,24},{9,... | collective-permute-start | bytes 98312 | tf_op jit(solution)/shard_map/ppermute | solution.py:14
  19.7 5.8 %collective-permute-start.3 = (f32[32,1,256]{2,1,0:T(1,128)S(1)}, f32[32,1,256]{2,1,0:T(1,128)S(1)}, u32[]{:S(2)}, u32[]{:S(2)}) collective-permute-start(f32[32,1,256]{2,1,0:T(1,128)S(1)} %get-tuple-element.55), channel_id=1, source_target_pairs={{16,0},{17,1},{18,2},{19,3},{20,4},{21,5},{22,6},{23,7},{24,8},{25... | collective-permute-start | bytes 98312 | tf_op jit(solution)/shard_map/ppermute | solution.py:17
  27.4 115.4 %all-reduce.17.cloned.1.call-start = ((), (), s32[]{:S(2)}) async-start(), calls=%async_computation.1 | async-start | bytes 524288
  60.7 4.3 %collective-permute-start.4 = (f32[32,2,256]{2,1,0:T(2,128)S(1)}, f32[32,2,256]{2,1,0:T(2,128)S(1)}, u32[]{:S(2)}, u32[]{:S(2)}) collective-permute-start(f32[32,2,256]{2,1,0:T(2,128)S(1)} %constant_dynamic-slice_fusion.3), channel_id=1, source_target_pairs={{0,1},{1,0},{2,3},{3,2},{4,5},{5,4},{6,7},{7,6},{8,9},{9,8},{10,11... | collective-permute-start | bytes 196616 | tf_op jit(solution)/shard_map/ppermute | solution.py:68
  65.9 5.2 %collective-permute-start.5 = (f32[32,2,256]{2,1,0:T(2,128)S(1)}, f32[32,2,256]{2,1,0:T(2,128)S(1)}, u32[]{:S(2)}, u32[]{:S(2)}) collective-permute-start(f32[32,2,256]{2,1,0:T(2,128)S(1)} %fusion.107), channel_id=1, source_target_pairs={{0,2},{1,3},{2,0},{3,1},{4,6},{5,7},{6,4},{7,5},{8,10},{9,11},{10,... | collective-permute-start | bytes 196616 | tf_op jit(solution)/shard_map/ppermute | solution.py:68
  100.1 5.0 %collective-permute-start.6 = (f32[32,1,256]{2,1,0:T(1,128)S(1)}, f32[32,1,256]{2,1,0:T(1,128)S(1)}, u32[]{:S(2)}, u32[]{:S(2)}) collective-permute-start(f32[32,1,256]{2,1,0:T(1,128)S(1)} %get-tuple-element.50), channel_id=1, source_target_pairs={{0,16},{1,17},{2,18},{3,19},{4,20},{5,21},{6,22},{7,23},{8,24},{9,... | collective-permute-start | bytes 98312 | tf_op jit(solution)/shard_map/ppermute | solution.py:14
  103.5 5.8 %collective-permute-start.7 = (f32[32,1,256]{2,1,0:T(1,128)S(1)}, f32[32,1,256]{2,1,0:T(1,128)S(1)}, u32[]{:S(2)}, u32[]{:S(2)}) collective-permute-start(f32[32,1,256]{2,1,0:T(1,128)S(1)} %get-tuple-element.51), channel_id=1, source_target_pairs={{16,0},{17,1},{18,2},{19,3},{20,4},{21,5},{22,6},{23,7},{24,8},{25... | collective-permute-start | bytes 98312 | tf_op jit(solution)/shard_map/ppermute | solution.py:17
  110.9 114.8 %all-reduce.19.cloned.1.call-start = ((), (), s32[]{:S(2)}) async-start(), calls=%async_computation.2 | async-start | bytes 524288
  143.6 4.3 %collective-permute-start.8 = (f32[32,2,256]{2,1,0:T(2,128)S(1)}, f32[32,2,256]{2,1,0:T(2,128)S(1)}, u32[]{:S(2)}, u32[]{:S(2)}) collective-permute-start(f32[32,2,256]{2,1,0:T(2,128)S(1)} %constant_dynamic-slice_fusion.2), channel_id=1, source_target_pairs={{0,1},{1,0},{2,3},{3,2},{4,5},{5,4},{6,7},{7,6},{8,9},{9,8},{10,11... | collective-permute-start | bytes 196616 | tf_op jit(solution)/shard_map/ppermute | solution.py:68
  148.8 5.2 %collective-permute-start.9 = (f32[32,2,256]{2,1,0:T(2,128)S(1)}, f32[32,2,256]{2,1,0:T(2,128)S(1)}, u32[]{:S(2)}, u32[]{:S(2)}) collective-permute-start(f32[32,2,256]{2,1,0:T(2,128)S(1)} %fusion.106), channel_id=1, source_target_pairs={{0,2},{1,3},{2,0},{3,1},{4,6},{5,7},{6,4},{7,5},{8,10},{9,11},{10,... | collective-permute-start | bytes 196616 | tf_op jit(solution)/shard_map/ppermute | solution.py:68
  182.9 5.0 %collective-permute-start.10 = (f32[32,1,256]{2,1,0:T(1,128)S(1)}, f32[32,1,256]{2,1,0:T(1,128)S(1)}, u32[]{:S(2)}, u32[]{:S(2)}) collective-permute-start(f32[32,1,256]{2,1,0:T(1,128)S(1)} %get-tuple-element.46), channel_id=1, source_target_pairs={{0,16},{1,17},{2,18},{3,19},{4,20},{5,21},{6,22},{7,23},{8,24},{9,... | collective-permute-start | bytes 98312 | tf_op jit(solution)/shard_map/ppermute | solution.py:14
  186.3 5.8 %collective-permute-start.11 = (f32[32,1,256]{2,1,0:T(1,128)S(1)}, f32[32,1,256]{2,1,0:T(1,128)S(1)}, u32[]{:S(2)}, u32[]{:S(2)}) collective-permute-start(f32[32,1,256]{2,1,0:T(1,128)S(1)} %get-tuple-element.47), channel_id=1, source_target_pairs={{16,0},{17,1},{18,2},{19,3},{20,4},{21,5},{22,6},{23,7},{24,8},{25... | collective-permute-start | bytes 98312 | tf_op jit(solution)/shard_map/ppermute | solution.py:17
  193.8 114.8 %all-reduce.21.cloned.1.call-start = ((), (), s32[]{:S(2)}) async-start(), calls=%async_computation.3 | async-start | bytes 524288
  226.5 4.3 %collective-permute-start.12 = (f32[32,2,256]{2,1,0:T(2,128)S(1)}, f32[32,2,256]{2,1,0:T(2,128)S(1)}, u32[]{:S(2)}, u32[]{:S(2)}) collective-permute-start(f32[32,2,256]{2,1,0:T(2,128)S(1)} %constant_dynamic-slice_fusion.1), channel_id=1, source_target_pairs={{0,1},{1,0},{2,3},{3,2},{4,5},{5,4},{6,7},{7,6},{8,9},{9,8},{10,11... | collective-permute-start | bytes 196616 | tf_op jit(solution)/shard_map/ppermute | solution.py:68
  231.7 5.2 %collective-permute-start.13 = (f32[32,2,256]{2,1,0:T(2,128)S(1)}, f32[32,2,256]{2,1,0:T(2,128)S(1)}, u32[]{:S(2)}, u32[]{:S(2)}) collective-permute-start(f32[32,2,256]{2,1,0:T(2,128)S(1)} %fusion.105), channel_id=1, source_target_pairs={{0,2},{1,3},{2,0},{3,1},{4,6},{5,7},{6,4},{7,5},{8,10},{9,11},{10,... | collective-permute-start | bytes 196616 | tf_op jit(solution)/shard_map/ppermute | solution.py:68
  265.8 5.0 %collective-permute-start.14 = (f32[32,1,256]{2,1,0:T(1,128)S(1)}, f32[32,1,256]{2,1,0:T(1,128)S(1)}, u32[]{:S(2)}, u32[]{:S(2)}) collective-permute-start(f32[32,1,256]{2,1,0:T(1,128)S(1)} %get-tuple-element.42), channel_id=1, source_target_pairs={{0,16},{1,17},{2,18},{3,19},{4,20},{5,21},{6,22},{7,23},{8,24},{9,... | collective-permute-start | bytes 98312 | tf_op jit(solution)/shard_map/ppermute | solution.py:14
  269.2 5.8 %collective-permute-start.15 = (f32[32,1,256]{2,1,0:T(1,128)S(1)}, f32[32,1,256]{2,1,0:T(1,128)S(1)}, u32[]{:S(2)}, u32[]{:S(2)}) collective-permute-start(f32[32,1,256]{2,1,0:T(1,128)S(1)} %get-tuple-element.43), channel_id=1, source_target_pairs={{16,0},{17,1},{18,2},{19,3},{20,4},{21,5},{22,6},{23,7},{24,8},{25... | collective-permute-start | bytes 98312 | tf_op jit(solution)/shard_map/ppermute | solution.py:17
  309.4 4.3 %collective-permute-start.16 = (f32[32,2,256]{2,1,0:T(2,128)S(1)}, f32[32,2,256]{2,1,0:T(2,128)S(1)}, u32[]{:S(2)}, u32[]{:S(2)}) collective-permute-start(f32[32,2,256]{2,1,0:T(2,128)S(1)} %constant_dynamic-slice_fusion), channel_id=1, source_target_pairs={{0,1},{1,0},{2,3},{3,2},{4,5},{5,4},{6,7},{7,6},{8,9},{9,8},{10,11... | collective-permute-start | bytes 196616 | tf_op jit(solution)/shard_map/ppermute | solution.py:68
  314.5 5.2 %collective-permute-start.17 = (f32[32,2,256]{2,1,0:T(2,128)S(1)}, f32[32,2,256]{2,1,0:T(2,128)S(1)}, u32[]{:S(2)}, u32[]{:S(2)}) collective-permute-start(f32[32,2,256]{2,1,0:T(2,128)S(1)} %fusion.104), channel_id=1, source_target_pairs={{0,2},{1,3},{2,0},{3,1},{4,6},{5,7},{6,4},{7,5},{8,10},{9,11},{10,... | collective-permute-start | bytes 196616 | tf_op jit(solution)/shard_map/ppermute | solution.py:68
  (2 other events, 5.0 us)
Sparse Core Ops, SparseCore 0:
  27.6 32.2 all-reduce.14
  111.0 31.7 all-reduce.16
  193.9 31.7 all-reduce.18
  276.8 31.7 all-reduce.20
